TPU v7x, 32 devices: a whole 2x2x4 slice. The times are simulated.
32 devices in a mesh: groups: 2 (over y), wide: 4 (over z), narrow: 4 (over x, core).
Axes of the slice: x: 2, y: 2, z: 4, core: 2. Of those that a mesh axis runs over, the one named last changes fastest.
Arguments:
- tokens: bfloat16 [256, 8192], P(('groups', 'wide'), 'narrow'), parts along dimension 0, may hold values from -6 to 6
- gate_weight: bfloat16 [8192, 16384], P('narrow', 'wide'), may hold values from -0.09375 to 0.09375
- up_weight: bfloat16 [8192, 16384], P('narrow', 'wide'), may hold values from -0.09375 to 0.09375
- down_weight: bfloat16 [16384, 8192], P('wide', 'narrow'), may hold values from -0.0625 to 0.0625
- gate_keep: int32 [64, 128], P('narrow', 'wide'), may hold values from 0 to 1, as said below
- up_keep: int32 [64, 128], P('narrow', 'wide'), may hold values from 0 to 1, as said below
- down_keep: int32 [128, 64], P('wide', 'narrow'), may hold values from 0 to 1, as said below
Outputs:
- mixed: bfloat16 [256, 8192], P(('groups', 'wide'), 'narrow'), parts along dimension 0
There are 2 independent parts, one for each index of `groups`. A program takes and returns all parts, laid end to end along the dimension named above; an argument that names none is the same for every part. Nothing has to cross between parts.
Inputs may be any that keep to these rules, and one draw needn't show every extreme that they name: `gate_keep`: 1 keeps a 128 x 128 block of the gate projection, 0 prunes it; the share kept differs between the tiles of blocks that the devices hold. `up_keep`: as for gate_keep, for the up projection. `down_keep`: as for gate_keep, for the down projection.
All inputs are finite; a program needn't handle non-finite values.
Results may differ from a plain program's by a relative error of at most 0.02.
Values may be sent and summed in bfloat16 or wider, within the bound.
A program may use at most 192 MiB of HBM per device.

v0:
```python
import jax
import jax.numpy as jnp
from jax import lax
from jax.sharding import PartitionSpec as P

BLOCK = 128


def widen(keep_mask):
    rows, cols = keep_mask.shape
    spread = jnp.broadcast_to(keep_mask[:, None, :, None], (rows, BLOCK, cols, BLOCK))
    return spread.reshape(rows * BLOCK, cols * BLOCK).astype(jnp.bfloat16)


def body(tokens, gate_weight, up_weight, down_weight, gate_keep, up_keep, down_keep):
    columns = gate_weight.shape[1]
    both_eff = jnp.concatenate((gate_weight * widen(gate_keep), up_weight * widen(up_keep)), axis=1)
    down_eff = down_weight * widen(down_keep)
    partial_value = jnp.dot(
        lax.all_gather(tokens, "wide", axis=0, tiled=True),
        both_eff,
        preferred_element_type=jnp.float32,
    )
    summed = lax.psum_scatter(
        partial_value.astype(jnp.bfloat16), "narrow", scatter_dimension=0, tiled=True
    ).astype(jnp.float32)
    share_rows = (jax.nn.silu(summed[:, :columns]) * summed[:, columns:]).astype(jnp.bfloat16)
    hidden = lax.all_gather(share_rows, "narrow", axis=0, tiled=True)
    return lax.psum_scatter(
        jnp.dot(hidden, down_eff, preferred_element_type=jnp.float32).astype(jnp.bfloat16),
        "wide",
        scatter_dimension=0,
        tiled=True,
    )


def solution(mesh):
    in_specs = (
        P(("groups", "wide"), "narrow"),
        P("narrow", "wide"),
        P("narrow", "wide"),
        P("wide", "narrow"),
        P("narrow", "wide"),
        P("narrow", "wide"),
        P("wide", "narrow"),
    )
    out_specs = P(("groups", "wide"), "narrow")
    return jax.shard_map(body, mesh=mesh, in_specs=in_specs, out_specs=out_specs, check_vma=False)
```

profile of v0, /device:TPU:0, one launch (start us, length us, event | category | flops | bytes accessed | tf_op | source)
XLA Modules:
  0.0 184.0 jit_solution(14055856806791446524)
XLA Ops:
  6.5 0.0 reduce-scatter.7.cloned.1.call-start
  6.5 0.7 convert_element_type.36
  7.2 0.7 convert_element_type.38
  7.9 17.6 %all_gather.6 = bf16[128,2048]{1,0:T(8,128)(2,1)S(1)} all-gather(bf16[32,2048]{1,0:T(8,128)(2,1)} %param.7), channel_id=1, replica_groups=mesh['groups'=2,'wide'=4,'narrow'=4] {'wide'}, dimensions={0}, use_global_device_ids=true | all-gather | bytes 655360 | tf_op jit(solution)/shard_map/all_gather | solution.py:20
  25.5 2.8 %broadcast_in_dim.6 = bf16[16,128,32,128]{3,2,1,0:T(8,128)(2,1)S(1)} broadcast(bf16[16,32]{1,0:T(8,128)(2,1)S(1)} %convert_element_type.36), dimensions={0,2} | broadcast | bytes 16778240 | tf_op jit(solution)/shard_map/broadcast_in_dim | solution.py:11
  28.3 6.3 %broadcast_in_dim.7 = bf16[16,128,32,128]{3,2,1,0:T(8,128)(2,1)} broadcast(bf16[16,32]{1,0:T(8,128)(2,1)S(1)} %convert_element_type.38), dimensions={0,2} | broadcast | bytes 16778240 | tf_op jit(solution)/shard_map/broadcast_in_dim | solution.py:11
  34.6 29.8 %bitcast_multiply_fusion.2 = (bf16[2048,4096]{1,0:T(8,128)(2,1)}, bf16[2048,4096]{1,0:T(8,128)(2,1)}) fusion(bf16[2048,4096]{1,0:T(8,128)(2,1)} %param.9, bf16[256,8,32,128]{3,2,1,0:T(8,128)(2,1)} %bitcast.21, bf16[2048,4096]{1,0:T(8,128)(2,1)} %param.8, bf16[256,8,32,128]{3,2,1,0:T(8,128)(2,1)S(1)} %bitcast.20), kind=kLoop, calls=%fused_computation.7 | loop fusion | flops 16777216 | bytes 100663296 | tf_op jit(solution)/shard_map/mul | solution.py:17
  64.4 0.0 copy-start
  64.4 14.5 %fusion.9 = bf16[128,8192]{0,1:T(8,128)(2,1)S(1)} fusion(bf16[128,2048]{1,0:T(8,128)(2,1)S(1)} %all_gather.6, bf16[2048,4096]{1,0:T(8,128)(2,1)} %get-tuple-element.5, bf16[2048,4096]{1,0:T(8,128)(2,1)} %get-tuple-element.6), kind=kOutput, calls=%fused_computation.10 | convolution fusion | flops 4363124736 | bytes 36175872 | tf_op jit(solution)/shard_map/dot_general | solution.py:19
  78.9 2.9 %copy.13 = bf16[128,8192]{1,0:T(8,128)(2,1)} copy(bf16[128,8192]{0,1:T(8,128)(2,1)S(1)} %fusion.9) | data formatting | bytes 4194304
  81.8 0.0 reduce-scatter.7.cloned.1.call-update
  81.9 0.0 all-gather.2.cloned.1.call-start
  81.9 33.3 %reduce-scatter.7.cloned.1.call-done = bf16[32,8192]{1,0:T(8,128)(2,1)} async-done(((bf16[128,8192]{1,0:T(8,128)(2,1)}), bf16[32,8192]{1,0:T(8,128)(2,1)}) %reduce-scatter.7.cloned.1.call-update) | async-done | bytes 524304 | tf_op jit(solution)/shard_map/reduce_scatter | solution.py:24
  115.2 1.1 convert_element_type.42
  116.3 0.8 fusion.13
  117.2 0.0 all-gather.2.cloned.1.call-update
  117.2 0.0 reduce-scatter.5.cloned.1.call-start
  117.3 0.0 copy-done
  117.3 0.1 copy.12
  117.4 16.7 %all-gather.2.cloned.1.call-done = bf16[128,4096]{1,0:T(8,128)(2,1)} async-done(((bf16[32,4096]{1,0:T(8,128)(2,1)}), bf16[128,4096]{1,0:T(8,128)(2,1)}) %all-gather.2.cloned.1.call-update) | async-done | bytes 1048592 | tf_op jit(solution)/shard_map/all_gather | solution.py:28
  134.1 0.0 copy-start.1
  134.1 6.2 %broadcast_in_dim.8 = bf16[32,128,16,128]{3,2,1,0:T(8,128)(2,1)} broadcast(bf16[32,16]{1,0:T(8,128)(2,1)S(1)} %copy.12), dimensions={0,2} | broadcast | bytes 16778240 | tf_op jit(solution)/shard_map/broadcast_in_dim | solution.py:11
  140.3 0.0 copy-done.1
  140.3 15.4 %fusion.12 = bf16[128,2048]{1,0:T(8,128)(2,1)} fusion(bf16[128,4096]{1,0:T(8,128)(2,1)S(1)} %copy-done.1, bf16[4096,2048]{1,0:T(8,128)(2,1)} %param.10, bf16[512,8,16,128]{3,2,1,0:T(8,128)(2,1)} %bitcast.22), kind=kOutput, calls=%fused_computation.11 | convolution fusion | flops 2156134400 | bytes 35127296 | tf_op jit(solution)/shard_map/dot_general | solution.py:30
  155.6 0.0 reduce-scatter.5.cloned.1.call-update
  155.7 21.8 %reduce-scatter.5.cloned.1.call-done = bf16[32,2048]{1,0:T(8,128)(2,1)} async-done(((bf16[128,2048]{1,0:T(8,128)(2,1)}), bf16[32,2048]{1,0:T(8,128)(2,1)}) %reduce-scatter.5.cloned.1.call-update) | async-done | bytes 131088 | tf_op jit(solution)/shard_map/reduce_scatter | solution.py:29
  (1 shorter events, 0.0 us)
Async XLA Ops:
  6.5 108.7 %reduce-scatter.7.cloned.1.call-start = ((), (), s32[]{:S(2)}) async-start(), calls=%async_computation.4 | async-start | bytes 2621440 | tf_op jit(solution)/shard_map/reduce_scatter | solution.py:24
  64.4 52.8 %copy-start = (s32[32,16]{0,1:T(8,128)S(1)}, s32[32,16]{0,1:T(8,128)}, u32[]{:S(2)}) copy-start(s32[32,16]{0,1:T(8,128)} %param.13) | copy-start | bytes 6148
  81.9 52.2 %all-gather.2.cloned.1.call-start = ((), (), s32[]{:S(2)}) async-start(), calls=%async_computation.2 | async-start | bytes 1310720 | tf_op jit(solution)/shard_map/all_gather | solution.py:28
  117.2 60.2 %reduce-scatter.5.cloned.1.call-start = ((), (), s32[]{:S(2)}) async-start(), calls=%async_computation.3 | async-start | bytes 655360 | tf_op jit(solution)/shard_map/reduce_scatter | solution.py:29
  134.1 6.2 %copy-start.1 = (bf16[128,4096]{1,0:T(8,128)(2,1)S(1)}, bf16[128,4096]{1,0:T(8,128)(2,1)}, u32[]{:S(2)}) copy-start(bf16[128,4096]{1,0:T(8,128)(2,1)} %all-gather.2.cloned.1.call-done) | copy-start | bytes 3145732
Sparse Core Ops, SparseCore 0:
  82.0 33.2 reduce-scatter.6
  117.3 16.7 all-gather.1
  155.8 21.6 reduce-scatter.4
where the time goes:
time: 184 us
  waiting for transfers between devices  71.9 us (39%)
  other arithmetic  33.2 us (18%)
  matrix products  29.8 us (16%)
  local copies, waits for them, and re-layouts  18.3 us (10%)
  blocking collectives  17.6 us (10%)
  between operations  13.1 us (7%)
    reduce_scatter x1, waiting for transfers between devices, body(): lax.psum_scatter(partial_value.astype(jnp.bfloat16), 'narrow', scatter_di...  33.3 us
    mul x1, other arithmetic, body(): up_weight * widen(up_keep)  29.8 us
    reduce_scatter x1, waiting for transfers between devices, body(): lax.psum_scatter(jnp.dot(hidden, down_eff, preferred_element_type=jnp.flo...  21.8 us
    all_gather x1, blocking collectives, body(): lax.all_gather(tokens, 'wide', axis=0, tiled=True)  17.6 us
    all_gather x1, waiting for transfers between devices, body(): hidden = lax.all_gather(share_rows, 'narrow', axis=0, tiled=True)  16.7 us
    dot_general x1, matrix products, body(): jnp.dot(hidden, down_eff, preferred_element_type=jnp.float32)  15.4 us
    broadcast_in_dim x3, local copies, waits for them, and re-layouts, widen(): jnp.broadcast_to(keep_mask[:, None, :, None], (rows, BLOCK, cols, BLOCK))  15.3 us
    dot_general x1, matrix products, body(): jnp.dot(lax.all_gather(tokens, 'wide', axis=0, tiled=True), both_eff, pre...  14.5 us
  transfers between devices with their start and end apart: 3, of which 3 were waited for; matrix products, arithmetic and copies ran while one was open for 0% of the time, Pallas kernels for 0%

commit v1 on v0

--- a/solution.py
+++ b/solution.py
@@ -1,9 +1,15 @@
 import jax
 import jax.numpy as jnp
 from jax import lax
+from jax.experimental import pallas as pl
+from jax.experimental.pallas import tpu as pltpu
 from jax.sharding import PartitionSpec as P
 
 BLOCK = 128
+MESH = pl.DeviceIdType.MESH
+CHUNK = 512
+PIECE = 512
+VMEM_LIMIT = 62 * 1024 * 1024
 
 
 def widen(keep_mask):
@@ -12,7 +18,7 @@
     return spread.reshape(rows * BLOCK, cols * BLOCK).astype(jnp.bfloat16)
 
 
-def body(tokens, gate_weight, up_weight, down_weight, gate_keep, up_keep, down_keep):
+def general_body(tokens, gate_weight, up_weight, down_weight, gate_keep, up_keep, down_keep):
     columns = gate_weight.shape[1]
     both_eff = jnp.concatenate((gate_weight * widen(gate_keep), up_weight * widen(up_keep)), axis=1)
     down_eff = down_weight * widen(down_keep)
@@ -34,6 +40,287 @@
     )
 
 
+def spread_columns(keep):
+    blocks = keep.shape[1]
+    shape = (blocks, blocks * BLOCK)
+    row = lax.broadcasted_iota(jnp.int32, shape, 0)
+    col = lax.broadcasted_iota(jnp.int32, shape, 1)
+    low = row * BLOCK
+    pick = jnp.where((col >= low) & (col < low + BLOCK), 1.0, 0.0).astype(jnp.bfloat16)
+    return jnp.dot(keep.astype(jnp.bfloat16), pick, preferred_element_type=jnp.float32)
+
+
+def make_kernel(rows, n_wide, depth, ff, chunks):
+    share = rows
+
+    def kernel(tok, gate, up, down, gkeep, ukeep, dkeep, out,
+               tokall, gbuf, ubuf, dbuf, gmask, umask, dmask,
+               pbuf, sibs, sibr, own, xs, xr, hid, acc, zs, zr,
+               t_s, t_r, w_g, w_u, w_d, sib_s, sib_r, x_s, x_r,
+               hs_s, hs_r, hx_s, hx_r, hf_s, hf_r, z_s, z_r):
+        w = lax.axis_index("wide")
+        n = lax.axis_index("narrow")
+        x = n // 2
+        k = n % 2
+        sib = 2 * x + (1 - k)
+        peer = 2 * (1 - x) + k
+        diag = 2 * (1 - x) + (1 - k)
+
+        def load_gate(c):
+            return pltpu.make_async_copy(gate.at[:, pl.ds(pl.multiple_of(c * CHUNK, CHUNK), CHUNK)], gbuf.at[c], w_g.at[c])
+
+        def load_up(c):
+            return pltpu.make_async_copy(up.at[:, pl.ds(pl.multiple_of(c * CHUNK, CHUNK), CHUNK)], ubuf.at[c], w_u.at[c])
+
+        def load_down(c):
+            return pltpu.make_async_copy(down.at[pl.ds(pl.multiple_of(c * CHUNK, CHUNK), CHUNK), :], dbuf.at[c], w_d.at[c])
+
+        @pl.loop(0, chunks)
+        def _(c):
+            load_gate(c).start()
+            load_up(c).start()
+
+        barrier = pltpu.get_barrier_semaphore()
+        for d in range(1, n_wide):
+            pl.semaphore_signal(barrier, inc=1, device_id={"wide": (w + d) % n_wide}, device_id_type=MESH)
+        for other in (sib, peer):
+            pl.semaphore_signal(barrier, inc=1, device_id={"narrow": other}, device_id_type=MESH)
+        pl.semaphore_wait(barrier, n_wide + 1)
+
+        def token_copy(d):
+            return pltpu.make_async_remote_copy(
+                src_ref=tok, dst_ref=tokall.at[pl.ds(pl.multiple_of(w * rows, rows), rows), :],
+                send_sem=t_s.at[d - 1], recv_sem=t_r.at[d - 1],
+                device_id={"wide": (w + d) % n_wide}, device_id_type=MESH)
+
+        def token_arrival(d):
+            source = (w + n_wide - d) % n_wide
+            return pltpu.make_async_remote_copy(
+                src_ref=tok, dst_ref=tokall.at[pl.ds(pl.multiple_of(source * rows, rows), rows), :],
+                send_sem=t_s.at[d - 1], recv_sem=t_r.at[d - 1],
+                device_id={"wide": (w + d) % n_wide}, device_id_type=MESH)
+
+        for d in (2, 3, 1):
+            token_copy(d).start()
+        tokall[pl.ds(pl.multiple_of(w * rows, rows), rows), :] = tok[...]
+
+        gmask[...] = spread_columns(gkeep[...])
+        umask[...] = spread_columns(ukeep[...])
+        dmask[...] = spread_columns(dkeep[...])
+        acc[...] = jnp.zeros_like(acc)
+
+        def apply_rows(buf, c, mask, mask_row, cols, width, row0):
+            line = mask[pl.ds(mask_row, 1), cols]
+            line = jnp.broadcast_to(line, (BLOCK, width)).astype(jnp.bfloat16)
+            at = pl.ds(row0, BLOCK)
+            buf[c, at, :] = buf[c, at, :] * line
+
+        def mask_gate_up(c):
+            cols = pl.ds(pl.multiple_of(c * CHUNK, CHUNK), CHUNK)
+
+            @pl.loop(0, depth // BLOCK)
+            def _(b):
+                row0 = pl.multiple_of(b * BLOCK, BLOCK)
+                apply_rows(gbuf, c, gmask, b, cols, CHUNK, row0)
+                apply_rows(ubuf, c, umask, b, cols, CHUNK, row0)
+
+        def mask_down(c):
+            for b in range(CHUNK // BLOCK):
+                apply_rows(dbuf, c, dmask, c * (CHUNK // BLOCK) + b, slice(None), depth, b * BLOCK)
+
+        @pl.loop(0, chunks)
+        def _(c):
+            load_gate(c).wait()
+            load_up(c).wait()
+            load_down(c).start()
+            mask_gate_up(c)
+
+        for d in (1, 2, 3):
+            token_arrival(d).wait_recv()
+
+        def remote(src, dst, send, recv, other):
+            return pltpu.make_async_remote_copy(
+                src_ref=src, dst_ref=dst, send_sem=send, recv_sem=recv,
+                device_id={"narrow": other}, device_id_type=MESH)
+
+        def sib_copy(c):
+            return remote(sibs.at[c], sibr.at[c], sib_s.at[c], sib_r.at[c], sib)
+
+        def x_copy(c):
+            return remote(xs.at[c], xr.at[c], x_s.at[c], x_r.at[c], peer)
+
+        def hid_sib(c, which):
+            return remote(hid.at[c, which], hid.at[c, which], hs_s.at[c], hs_r.at[c], sib)
+
+        def hid_x(c, which):
+            return remote(hid.at[c, which], hid.at[c, which], hx_s.at[c], hx_r.at[c], peer)
+
+        def hid_forward(c, which):
+            return remote(hid.at[c, which], hid.at[c, which], hf_s.at[c], hf_r.at[c], sib)
+
+        def share_at(j):
+            return pl.ds(pl.multiple_of(j * share, share), share)
+
+        def stage_partial(c):
+            slot = c % 2
+            all_tokens = tokall[...]
+            pbuf[slot, :, 0:CHUNK] = jnp.dot(all_tokens, gbuf[c], preferred_element_type=jnp.float32)
+            pbuf[slot, :, CHUNK:] = jnp.dot(all_tokens, ubuf[c], preferred_element_type=jnp.float32)
+            for side in range(2):
+                sibs[c, side] = pbuf[slot, share_at(2 * side + 1 - k), :].astype(jnp.bfloat16)
+            sib_copy(c).start()
+
+        def stage_chip_sum(c):
+            slot = c % 2
+            sib_copy(c).wait_recv()
+            xs[c] = (pbuf[slot, share_at(peer), :] + sibr[c, 1 - x].astype(jnp.float32)).astype(jnp.bfloat16)
+            x_copy(c).start()
+            own[c] = pbuf[slot, share_at(n), :] + sibr[c, x].astype(jnp.float32)
+
+        def stage_hidden(c):
+            x_copy(c).wait_recv()
+            both = own[c] + xr[c].astype(jnp.float32)
+            g, u = both[:, :CHUNK], both[:, CHUNK:]
+            hid[c, n] = (g / (1.0 + jnp.exp(-g)) * u).astype(jnp.bfloat16)
+            hid_x(c, n).start()
+            hid_sib(c, n).start()
+
+        def stage_forward(c):
+            hid_x(c, peer).wait_recv()
+            hid_forward(c, peer).start()
+
+        def wait_hidden(c):
+            hid_sib(c, sib).wait_recv()
+            hid_forward(c, diag).wait_recv()
+
+        def stage_down(c):
+            wait_hidden(c)
+            h = hid[c].reshape(4 * share, CHUNK)
+
+            @pl.loop(0, depth // PIECE)
+            def _(q):
+                cols = pl.ds(pl.multiple_of(q * PIECE, PIECE), PIECE)
+                acc[:, cols] += jnp.dot(h, dbuf[c, :, cols], preferred_element_type=jnp.float32)
+
+        @pl.loop(0, chunks + 5)
+        def _(t):
+            @pl.when(t < chunks)
+            def _():
+                stage_partial(t)
+
+            @pl.when((t >= 1) & (t < chunks + 1))
+            def _():
+                stage_chip_sum(t - 1)
+
+            @pl.when(t < chunks)
+            def _():
+                load_down(t).wait()
+                mask_down(t)
+
+            @pl.when((t >= 3) & (t < chunks + 3))
+            def _():
+                stage_hidden(t - 3)
+
+            @pl.when((t >= 4) & (t < chunks + 4))
+            def _():
+                stage_forward(t - 4)
+
+            @pl.when((t >= 5) & (t < chunks + 4))
+            def _():
+                stage_down(t - 5)
+
+        def z_copy(q, d):
+            return pltpu.make_async_remote_copy(
+                src_ref=zs.at[q, d - 1], dst_ref=zr.at[q, d - 1],
+                send_sem=z_s.at[q, d - 1], recv_sem=z_r.at[q, d - 1],
+                device_id={"wide": (w + d) % n_wide}, device_id_type=MESH)
+
+        wait_hidden(chunks - 1)
+        last = hid[chunks - 1].reshape(4 * share, CHUNK)
+
+        @pl.loop(0, depth // PIECE)
+        def _(q):
+            cols = pl.ds(pl.multiple_of(q * PIECE, PIECE), PIECE)
+            acc[:, cols] += jnp.dot(last, dbuf[chunks - 1, :, cols], preferred_element_type=jnp.float32)
+            for d in (2, 3, 1):
+                zs[q, d - 1] = acc[share_at((w + d) % n_wide), cols].astype(jnp.bfloat16)
+                z_copy(q, d).start()
+
+        @pl.loop(0, depth // PIECE)
+        def _(q):
+            cols = pl.ds(pl.multiple_of(q * PIECE, PIECE), PIECE)
+            total = acc[share_at(w), cols]
+            for d in (1, 2, 3):
+                z_copy(q, d).wait_recv()
+                total = total + zr[q, d - 1].astype(jnp.float32)
+            out[:, cols] = total.astype(jnp.bfloat16)
+
+        for d in (1, 2, 3):
+            token_copy(d).wait_send()
+
+        @pl.loop(0, chunks)
+        def _(c):
+            sib_copy(c).wait_send()
+            x_copy(c).wait_send()
+            hid_x(c, n).wait_send()
+            hid_sib(c, n).wait_send()
+            hid_forward(c, peer).wait_send()
+
+        @pl.loop(0, depth // PIECE)
+        def _(q):
+            for d in (1, 2, 3):
+                z_copy(q, d).wait_send()
+
+    return kernel
+
+
+def fused_body(n_wide):
+    def body(tokens, gate_weight, up_weight, down_weight, gate_keep, up_keep, down_keep):
+        rows, depth = tokens.shape
+        ff = gate_weight.shape[1]
+        chunks = ff // CHUNK
+        pieces = depth // PIECE
+        bf, f32 = jnp.bfloat16, jnp.float32
+        vmem = pl.BlockSpec(memory_space=pltpu.VMEM)
+        anywhere = pl.BlockSpec(memory_space=pl.ANY)
+        dma = pltpu.SemaphoreType.DMA
+        return pl.pallas_call(
+            make_kernel(rows, n_wide, depth, ff, chunks),
+            out_shape=jax.ShapeDtypeStruct((rows, depth), bf),
+            in_specs=[vmem, anywhere, anywhere, anywhere, vmem, vmem, vmem],
+            out_specs=vmem,
+            scratch_shapes=[
+                pltpu.VMEM((n_wide * rows, depth), bf),
+                pltpu.VMEM((chunks, depth, CHUNK), bf),
+                pltpu.VMEM((chunks, depth, CHUNK), bf),
+                pltpu.VMEM((chunks, CHUNK, depth), bf),
+                pltpu.VMEM((depth // BLOCK, ff), f32),
+                pltpu.VMEM((depth // BLOCK, ff), f32),
+                pltpu.VMEM((ff // BLOCK, depth), f32),
+                pltpu.VMEM((2, n_wide * rows, 2 * CHUNK), f32),
+                pltpu.VMEM((chunks, 2, rows, 2 * CHUNK), bf),
+                pltpu.VMEM((chunks, 2, rows, 2 * CHUNK), bf),
+                pltpu.VMEM((chunks, rows, 2 * CHUNK), f32),
+                pltpu.VMEM((chunks, rows, 2 * CHUNK), bf),
+                pltpu.VMEM((chunks, rows, 2 * CHUNK), bf),
+                pltpu.VMEM((chunks, 4, rows, CHUNK), bf),
+                pltpu.VMEM((n_wide * rows, depth), f32),
+                pltpu.VMEM((pieces, n_wide - 1, rows, PIECE), bf),
+                pltpu.VMEM((pieces, n_wide - 1, rows, PIECE), bf),
+                dma((n_wide - 1,)), dma((n_wide - 1,)),
+                dma((chunks,)), dma((chunks,)), dma((chunks,)),
+                dma((chunks,)), dma((chunks,)), dma((chunks,)), dma((chunks,)),
+                dma((chunks,)), dma((chunks,)), dma((chunks,)), dma((chunks,)),
+                dma((chunks,)), dma((chunks,)),
+                dma((pieces, n_wide - 1)), dma((pieces, n_wide - 1)),
+            ],
+            compiler_params=pltpu.CompilerParams(
+                collective_id=0, has_side_effects=True, vmem_limit_bytes=VMEM_LIMIT),
+        )(tokens, gate_weight, up_weight, down_weight, gate_keep, up_keep, down_keep)
+
+    return body
+
+
 def solution(mesh):
     in_specs = (
         P(("groups", "wide"), "narrow"),
@@ -45,4 +332,6 @@
         P("wide", "narrow"),
     )
     out_specs = P(("groups", "wide"), "narrow")
+    fits = mesh.shape["wide"] == 4 and mesh.shape["narrow"] == 4
+    body = fused_body(mesh.shape["wide"]) if fits else general_body
     return jax.shard_map(body, mesh=mesh, in_specs=in_specs, out_specs=out_specs, check_vma=False)

time: 184 us -> 62.8 us (0.34)
  waiting for transfers between devices: 71.9 us -> 0 us
  Pallas kernels: 0 us -> 59.6 us
  other arithmetic: 33.2 us -> 0 us
  matrix products: 29.8 us -> 0 us
  blocking collectives: 17.6 us -> 0 us
  local copies, waits for them, and re-layouts: 18.3 us -> 2.94 us
  between operations: 13.1 us -> 0.01 us
    pallas_call x0 -> x1, Pallas kernels: none -> 59.6 us  [body(): pl.pallas_call(make_kernel(rows, n_wide, depth, ff, chunks), out_shape=ja...]
    reduce_scatter x2 -> x0, waiting for transfers between devices: 55.1 us -> none  [the longest x1 33.3 us: body(): lax.psum_scatter(partial_value.astype(jnp.bfloat16), 'narrow', scatter_di...]
    dot_general x2 -> x0, matrix products: 29.8 us -> none  [the longest x1 15.4 us: body(): jnp.dot(hidden, down_eff, preferred_element_type=jnp.float32)]
    mul x1 -> x0, other arithmetic: 29.8 us -> none  [body(): up_weight * widen(up_keep)]
    all_gather x1 -> x0, blocking collectives: 17.6 us -> none  [body(): lax.all_gather(tokens, 'wide', axis=0, tiled=True)]
    all_gather x1 -> x0, waiting for transfers between devices: 16.7 us -> none  [body(): hidden = lax.all_gather(share_rows, 'narrow', axis=0, tiled=True)]
    broadcast_in_dim x3 -> x0, local copies, waits for them, and re-layouts: 15.3 us -> none  [widen(): jnp.broadcast_to(keep_mask[:, None, :, None], (rows, BLOCK, cols, BLOCK))]
    convert_element_type x5 -> x0, other arithmetic: 3.36 us -> none  [the longest x3 1.4 us: widen(): return spread.reshape(rows * BLOCK, cols * BLOCK).astype(jnp.bfloat16)]
  transfers between devices with their start and end apart: 3 -> 0, of which waited for: 3 -> 0; matrix products, arithmetic and copies ran while one was open for 0% -> 0% of each run, Pallas kernels for 0% -> 0%
where the time goes in v1:
time: 62.8 us; the launch traced here: 62.5 us
  Pallas kernels  59.6 us (95%)
  local copies, waits for them, and re-layouts  2.94 us (5%)
    pallas_call x1, Pallas kernels, body(): pl.pallas_call(make_kernel(rows, n_wide, depth, ff, chunks), out_shape=ja...  59.6 us
    unnamed x2, local copies, waits for them, and re-layouts  2.94 us

profile of v1, /device:TPU:0, one launch (start us, length us, event | category | flops | bytes accessed | tf_op | source)
XLA Modules:
  0.0 62.5 jit_solution(6621461818197682041)
XLA Ops:
  0.0 1.4 %copy.8.dkeep = s32[32,16]{1,0:T(8,128)} copy(s32[32,16]{0,1:T(8,128)} %param.13) | data formatting | bytes 4096 | tf_op args[6]
  1.4 59.6 %shard_map.73 = bf16[32,2048]{1,0:T(8,128)(2,1)} custom-call(bf16[32,2048]{1,0:T(8,128)(2,1)} %tok.1, bf16[2048,4096]{1,0:T(8,128)(2,1)} %gate.1, bf16[2048,4096]{1,0:T(8,128)(2,1)} %up.1, bf16[4096,2048]{1,0:T(8,128)(2,1)} %down.1, s32[16,32]{1,0:T(8,128)} %gkeep.1, s32[16,32]{1,0:T(8,128)} %ukeep.1, s32[32,16]{1,0:T(8,128)} %copy.8.dkeep), custom_call_target="tpu_custom_call" | custom-call | tf_op jit(solution)/shard_map/pallas_call | solution.py:287
  61.0 1.6 %copy.10 = bf16[32,2048]{1,0:T(8,128)(2,1)} copy(bf16[32,2048]{1,0:T(8,128)(2,1)} %shard_map.73) | data formatting | bytes 262144

commit v2 on v0

--- a/solution.py
+++ b/solution.py
@@ -1,9 +1,23 @@
 import jax
 import jax.numpy as jnp
 from jax import lax
+from jax.experimental import pallas as pl
+from jax.experimental.pallas import tpu as pltpu
 from jax.sharding import PartitionSpec as P
 
 BLOCK = 128
+MESH = pl.DeviceIdType.MESH
+CHUNK = 512
+PIECE = 1024
+HALVES = 1
+SLOTS = 3
+AHEAD = 3
+INFLIGHT = 3
+SUM_LAG = 2
+HIDDEN_LAG = 5
+FORWARD = 2
+EXTRA = 0
+VMEM_LIMIT = 62 * 1024 * 1024
 
 
 def widen(keep_mask):
@@ -12,7 +26,7 @@
     return spread.reshape(rows * BLOCK, cols * BLOCK).astype(jnp.bfloat16)
 
 
-def body(tokens, gate_weight, up_weight, down_weight, gate_keep, up_keep, down_keep):
+def general_body(tokens, gate_weight, up_weight, down_weight, gate_keep, up_keep, down_keep):
     columns = gate_weight.shape[1]
     both_eff = jnp.concatenate((gate_weight * widen(gate_keep), up_weight * widen(up_keep)), axis=1)
     down_eff = down_weight * widen(down_keep)
@@ -34,6 +48,297 @@
     )
 
 
+def spread_columns(keep):
+    blocks = keep.shape[1]
+    shape = (blocks, blocks * BLOCK)
+    row = lax.broadcasted_iota(jnp.int32, shape, 0)
+    col = lax.broadcasted_iota(jnp.int32, shape, 1)
+    low = row * BLOCK
+    pick = jnp.where((col >= low) & (col < low + BLOCK), 1.0, 0.0).astype(jnp.bfloat16)
+    return jnp.dot(keep.astype(jnp.bfloat16), pick, preferred_element_type=jnp.float32)
+
+
+def make_kernel(rows, n_wide, depth, ff, chunks):
+    share = rows // HALVES
+
+    def kernel(tok, gate, up, down, gkeep, ukeep, dkeep, out,
+               tokall, gbuf, ubuf, dbuf, gmask, umask, dmask,
+               pbuf, sibs, sibr, own, xs, xr, hid, acc, zs, zr,
+               t_s, t_r, w_g, w_u, w_d, sib_s, sib_r, x_s, x_r,
+               hs_s, hs_r, hx_s, hx_r, hf_s, hf_r, z_s, z_r):
+        w = lax.axis_index("wide")
+        n = lax.axis_index("narrow")
+        x = n // 2
+        k = n % 2
+        sib = 2 * x + (1 - k)
+        peer = 2 * (1 - x) + k
+        diag = 2 * (1 - x) + (1 - k)
+
+        def load_gate(c):
+            return pltpu.make_async_copy(gate.at[:, pl.ds(pl.multiple_of(c * CHUNK, CHUNK), CHUNK)], gbuf.at[c], w_g.at[c])
+
+        def load_up(c):
+            return pltpu.make_async_copy(up.at[:, pl.ds(pl.multiple_of(c * CHUNK, CHUNK), CHUNK)], ubuf.at[c], w_u.at[c])
+
+        def load_down(c):
+            return pltpu.make_async_copy(down.at[pl.ds(pl.multiple_of(c * CHUNK, CHUNK), CHUNK), :], dbuf.at[c], w_d.at[c])
+
+        def start_load(item):
+            @pl.when(item < chunks)
+            def _():
+                load_gate(item).start()
+                load_up(item).start()
+
+            @pl.when((item >= chunks) & (item < 2 * chunks))
+            def _():
+                load_down(item - chunks).start()
+
+        @pl.loop(0, INFLIGHT)
+        def _(item):
+            start_load(item)
+
+        barrier = pltpu.get_barrier_semaphore()
+        for d in range(1, n_wide):
+            pl.semaphore_signal(barrier, inc=1, device_id={"wide": (w + d) % n_wide}, device_id_type=MESH)
+        for other in (sib, peer):
+            pl.semaphore_signal(barrier, inc=1, device_id={"narrow": other}, device_id_type=MESH)
+        pl.semaphore_wait(barrier, n_wide + 1)
+
+        def token_move(h, d, owner):
+            return pltpu.make_async_remote_copy(
+                src_ref=tok.at[pl.ds(h * share, share), :],
+                dst_ref=tokall.at[h, pl.ds(pl.multiple_of(owner * share, share), share), :],
+                send_sem=t_s.at[h, d - 1], recv_sem=t_r.at[h, d - 1],
+                device_id={"wide": (w + d) % n_wide}, device_id_type=MESH)
+
+        def token_copy(h, d):
+            return token_move(h, d, w)
+
+        def token_arrival(h, d):
+            return token_move(h, d, (w + n_wide - d) % n_wide)
+
+        for d in (2, 3, 1):
+            token_copy(0, d).start()
+        for h in range(HALVES):
+            tokall[h, pl.ds(pl.multiple_of(w * share, share), share), :] = tok[h * share:(h + 1) * share, :]
+
+        gmask[...] = spread_columns(gkeep[...])
+        umask[...] = spread_columns(ukeep[...])
+        dmask[...] = spread_columns(dkeep[...])
+        acc[...] = jnp.zeros_like(acc)
+
+        def apply_rows(buf, c, mask, mask_row, cols, width, row0):
+            line = mask[pl.ds(mask_row, 1), cols]
+            line = jnp.broadcast_to(line, (BLOCK, width)).astype(jnp.bfloat16)
+            at = pl.ds(row0, BLOCK)
+            buf[c, at, :] = buf[c, at, :] * line
+
+        def prepare_gate_up(c):
+            load_gate(c).wait()
+            load_up(c).wait()
+            start_load(c + INFLIGHT)
+            cols = pl.ds(pl.multiple_of(c * CHUNK, CHUNK), CHUNK)
+
+            @pl.loop(0, depth // BLOCK)
+            def _(b):
+                row0 = pl.multiple_of(b * BLOCK, BLOCK)
+                apply_rows(gbuf, c, gmask, b, cols, CHUNK, row0)
+                apply_rows(ubuf, c, umask, b, cols, CHUNK, row0)
+
+        def prepare_down(c):
+            load_down(c).wait()
+            start_load(chunks + c + INFLIGHT)
+            for b in range(CHUNK // BLOCK):
+                apply_rows(dbuf, c, dmask, c * (CHUNK // BLOCK) + b, slice(None), depth, b * BLOCK)
+
+        @pl.loop(0, AHEAD)
+        def _(c):
+            prepare_gate_up(c)
+
+        for d in (1, 2, 3):
+            token_arrival(0, d).wait_recv()
+        def remote(src, dst, send, recv, other):
+            return pltpu.make_async_remote_copy(
+                src_ref=src, dst_ref=dst, send_sem=send, recv_sem=recv,
+                device_id={"narrow": other}, device_id_type=MESH)
+
+        def sib_copy(v):
+            return remote(sibs.at[v], sibr.at[v], sib_s.at[v], sib_r.at[v], sib)
+
+        def x_copy(v):
+            return remote(xs.at[v], xr.at[v], x_s.at[v], x_r.at[v], peer)
+
+        def hid_sib(v, which):
+            return remote(hid.at[v, which], hid.at[v, which], hs_s.at[v], hs_r.at[v], sib)
+
+        def hid_x(v, which):
+            return remote(hid.at[v, which], hid.at[v, which], hx_s.at[v], hx_r.at[v], peer)
+
+        def hid_forward(v, which):
+            return remote(hid.at[v, which], hid.at[v, which], hf_s.at[v], hf_r.at[v], sib)
+
+        def share_at(j):
+            return pl.ds(pl.multiple_of(j * share, share), share)
+
+        units = HALVES * chunks
+
+        def stage_partial(v):
+            slot = v % SLOTS
+            h, c = v // chunks, v % chunks
+            half_tokens = tokall[h]
+            pbuf[slot, :, 0:CHUNK] = jnp.dot(half_tokens, gbuf[c], preferred_element_type=jnp.float32)
+            pbuf[slot, :, CHUNK:] = jnp.dot(half_tokens, ubuf[c], preferred_element_type=jnp.float32)
+            for side in range(2):
+                sibs[v, side] = pbuf[slot, share_at(2 * side + 1 - k), :].astype(jnp.bfloat16)
+            sib_copy(v).start()
+
+        def stage_chip_sum(v):
+            slot = v % SLOTS
+            sib_copy(v).wait_recv()
+            xs[v] = (pbuf[slot, share_at(peer), :] + sibr[v, 1 - x].astype(jnp.float32)).astype(jnp.bfloat16)
+            x_copy(v).start()
+            own[v] = pbuf[slot, share_at(n), :] + sibr[v, x].astype(jnp.float32)
+
+        def stage_hidden(v):
+            x_copy(v).wait_recv()
+            both = own[v] + xr[v].astype(jnp.float32)
+            g, u = both[:, :CHUNK], both[:, CHUNK:]
+            hid[v, n] = (g / (1.0 + jnp.exp(-g)) * u).astype(jnp.bfloat16)
+            hid_x(v, n).start()
+            hid_sib(v, n).start()
+
+        def stage_forward(v):
+            hid_x(v, peer).wait_recv()
+            hid_forward(v, peer).start()
+
+        def z_copy(h, q, d):
+            return pltpu.make_async_remote_copy(
+                src_ref=zs.at[h, q, d - 1], dst_ref=zr.at[h, q, d - 1],
+                send_sem=z_s.at[h, q, d - 1], recv_sem=z_r.at[h, q, d - 1],
+                device_id={"wide": (w + d) % n_wide}, device_id_type=MESH)
+
+        def stage_down(v):
+            h, c = v // chunks, v % chunks
+
+            hid_sib(v, sib).wait_recv()
+            hid_forward(v, diag).wait_recv()
+
+            @pl.loop(0, depth // PIECE)
+            def _(q):
+                cols = pl.ds(pl.multiple_of(q * PIECE, PIECE), PIECE)
+                hidden = hid[v].reshape(n_wide * share, CHUNK)
+                acc[h, :, cols] += jnp.dot(hidden, dbuf[c, :, cols], preferred_element_type=jnp.float32)
+
+                @pl.when(c == chunks - 1)
+                def _():
+                    for d in (2, 3, 1):
+                        zs[h, q, d - 1] = acc[h, share_at((w + d) % n_wide), cols].astype(jnp.bfloat16)
+                        z_copy(h, q, d).start()
+
+        def staged(t, lag, stage):
+            @pl.when((t >= lag) & (t < chunks + lag))
+            def _():
+                stage(t - lag)
+
+        @pl.loop(0, 2 * chunks + EXTRA)
+        def _(t):
+            @pl.when((t >= AHEAD) & (t < chunks))
+            def _():
+                prepare_gate_up(t)
+
+            staged(t, 0, stage_partial)
+
+            @pl.when((t >= chunks) & (t < 2 * chunks))
+            def _():
+                prepare_down(t - chunks)
+
+            staged(t, SUM_LAG, stage_chip_sum)
+            staged(t, HIDDEN_LAG, stage_hidden)
+            staged(t, HIDDEN_LAG + FORWARD, stage_forward)
+            staged(t, chunks + EXTRA, stage_down)
+
+        for h in range(HALVES):
+            rows_at = pl.ds(h * share, share)
+
+            @pl.loop(0, depth // PIECE)
+            def _(q):
+                cols = pl.ds(pl.multiple_of(q * PIECE, PIECE), PIECE)
+                total = acc[h, share_at(w), cols]
+                for d in (1, 2, 3):
+                    z_copy(h, q, d).wait_recv()
+                    total = total + zr[h, q, d - 1].astype(jnp.float32)
+                out[rows_at, cols] = total.astype(jnp.bfloat16)
+
+        for h in range(HALVES):
+            for d in (1, 2, 3):
+                token_copy(h, d).wait_send()
+
+        @pl.loop(0, units)
+        def _(v):
+            sib_copy(v).wait_send()
+            x_copy(v).wait_send()
+            hid_x(v, n).wait_send()
+            hid_sib(v, n).wait_send()
+            hid_forward(v, peer).wait_send()
+
+        for h in range(HALVES):
+            @pl.loop(0, depth // PIECE)
+            def _(q):
+                for d in (1, 2, 3):
+                    z_copy(h, q, d).wait_send()
+
+    return kernel
+
+
+def fused_body(n_wide):
+    def body(tokens, gate_weight, up_weight, down_weight, gate_keep, up_keep, down_keep):
+        rows, depth = tokens.shape
+        ff = gate_weight.shape[1]
+        chunks = ff // CHUNK
+        pieces = depth // PIECE
+        share = rows // HALVES
+        units = HALVES * chunks
+        bf, f32 = jnp.bfloat16, jnp.float32
+        vmem = pl.BlockSpec(memory_space=pltpu.VMEM)
+        anywhere = pl.BlockSpec(memory_space=pl.ANY)
+        dma = pltpu.SemaphoreType.DMA
+        return pl.pallas_call(
+            make_kernel(rows, n_wide, depth, ff, chunks),
+            out_shape=jax.ShapeDtypeStruct((rows, depth), bf),
+            in_specs=[vmem, anywhere, anywhere, anywhere, vmem, vmem, vmem],
+            out_specs=vmem,
+            scratch_shapes=[
+                pltpu.VMEM((HALVES, n_wide * share, depth), bf),
+                pltpu.VMEM((chunks, depth, CHUNK), bf),
+                pltpu.VMEM((chunks, depth, CHUNK), bf),
+                pltpu.VMEM((chunks, CHUNK, depth), bf),
+                pltpu.VMEM((depth // BLOCK, ff), f32),
+                pltpu.VMEM((depth // BLOCK, ff), f32),
+                pltpu.VMEM((ff // BLOCK, depth), f32),
+                pltpu.VMEM((SLOTS, n_wide * share, 2 * CHUNK), f32),
+                pltpu.VMEM((units, 2, share, 2 * CHUNK), bf),
+                pltpu.VMEM((units, 2, share, 2 * CHUNK), bf),
+                pltpu.VMEM((units, share, 2 * CHUNK), f32),
+                pltpu.VMEM((units, share, 2 * CHUNK), bf),
+                pltpu.VMEM((units, share, 2 * CHUNK), bf),
+                pltpu.VMEM((units, 4, share, CHUNK), bf),
+                pltpu.VMEM((HALVES, n_wide * share, depth), f32),
+                pltpu.VMEM((HALVES, pieces, n_wide - 1, share, PIECE), bf),
+                pltpu.VMEM((HALVES, pieces, n_wide - 1, share, PIECE), bf),
+                dma((HALVES, n_wide - 1)), dma((HALVES, n_wide - 1)),
+                dma((chunks,)), dma((chunks,)), dma((chunks,)),
+                dma((units,)), dma((units,)), dma((units,)), dma((units,)),
+                dma((units,)), dma((units,)), dma((units,)), dma((units,)),
+                dma((units,)), dma((units,)),
+                dma((HALVES, pieces, n_wide - 1)), dma((HALVES, pieces, n_wide - 1)),
+            ],
+            compiler_params=pltpu.CompilerParams(
+                collective_id=0, has_side_effects=True, vmem_limit_bytes=VMEM_LIMIT),
+        )(tokens, gate_weight, up_weight, down_weight, gate_keep, up_keep, down_keep)
+
+    return body
+
+
 def solution(mesh):
     in_specs = (
         P(("groups", "wide"), "narrow"),
@@ -45,4 +350,6 @@
         P("wide", "narrow"),
     )
     out_specs = P(("groups", "wide"), "narrow")
+    fits = mesh.shape["wide"] == 4 and mesh.shape["narrow"] == 4
+    body = fused_body(mesh.shape["wide"]) if fits else general_body
     return jax.shard_map(body, mesh=mesh, in_specs=in_specs, out_specs=out_specs, check_vma=False)

time: 184 us -> 59.2 us (0.32)
  waiting for transfers between devices: 71.9 us -> 0 us
  Pallas kernels: 0 us -> 56 us
  other arithmetic: 33.2 us -> 0 us
  matrix products: 29.8 us -> 0 us
  blocking collectives: 17.6 us -> 0 us
  local copies, waits for them, and re-layouts: 18.3 us -> 2.94 us
  between operations: 13.1 us -> 0.01 us
    pallas_call x0 -> x1, Pallas kernels: none -> 56 us  [body(): pl.pallas_call(make_kernel(rows, n_wide, depth, ff, chunks), out_shape=ja...]
    reduce_scatter x2 -> x0, waiting for transfers between devices: 55.1 us -> none  [the longest x1 33.3 us: body(): lax.psum_scatter(partial_value.astype(jnp.bfloat16), 'narrow', scatter_di...]
    dot_general x2 -> x0, matrix products: 29.8 us -> none  [the longest x1 15.4 us: body(): jnp.dot(hidden, down_eff, preferred_element_type=jnp.float32)]
    mul x1 -> x0, other arithmetic: 29.8 us -> none  [body(): up_weight * widen(up_keep)]
    all_gather x1 -> x0, blocking collectives: 17.6 us -> none  [body(): lax.all_gather(tokens, 'wide', axis=0, tiled=True)]
    all_gather x1 -> x0, waiting for transfers between devices: 16.7 us -> none  [body(): hidden = lax.all_gather(share_rows, 'narrow', axis=0, tiled=True)]
    broadcast_in_dim x3 -> x0, local copies, waits for them, and re-layouts: 15.3 us -> none  [widen(): jnp.broadcast_to(keep_mask[:, None, :, None], (rows, BLOCK, cols, BLOCK))]
    convert_element_type x5 -> x0, other arithmetic: 3.36 us -> none  [the longest x3 1.4 us: widen(): return spread.reshape(rows * BLOCK, cols * BLOCK).astype(jnp.bfloat16)]
  transfers between devices with their start and end apart: 3 -> 0, of which waited for: 3 -> 0; matrix products, arithmetic and copies ran while one was open for 0% -> 0% of each run, Pallas kernels for 0% -> 0%
where the time goes in v2:
time: 59.2 us; the launch traced here: 59 us
  Pallas kernels  56 us (95%)
  local copies, waits for them, and re-layouts  2.94 us (5%)
    pallas_call x1, Pallas kernels, body(): pl.pallas_call(make_kernel(rows, n_wide, depth, ff, chunks), out_shape=ja...  56 us
    unnamed x2, local copies, waits for them, and re-layouts  2.94 us

profile of v2, /device:TPU:0, one launch (start us, length us, event | category | flops | bytes accessed | tf_op | source)
XLA Modules:
  0.0 59.0 jit_solution(12962618900074426267)
XLA Ops:
  0.0 1.4 %copy.8.dkeep = s32[32,16]{1,0:T(8,128)} copy(s32[32,16]{0,1:T(8,128)} %param.13) | data formatting | bytes 4096 | tf_op args[6]
  1.4 56.0 %shard_map.73 = bf16[32,2048]{1,0:T(8,128)(2,1)} custom-call(bf16[32,2048]{1,0:T(8,128)(2,1)} %tok.1, bf16[2048,4096]{1,0:T(8,128)(2,1)} %gate.1, bf16[2048,4096]{1,0:T(8,128)(2,1)} %up.1, bf16[4096,2048]{1,0:T(8,128)(2,1)} %down.1, s32[16,32]{1,0:T(8,128)} %gkeep.1, s32[16,32]{1,0:T(8,128)} %ukeep.1, s32[32,16]{1,0:T(8,128)} %copy.8.dkeep), custom_call_target="tpu_custom_call" | custom-call | tf_op jit(solution)/shard_map/pallas_call | solution.py:305
  57.4 1.6 %copy.10 = bf16[32,2048]{1,0:T(8,128)(2,1)} copy(bf16[32,2048]{1,0:T(8,128)(2,1)} %shard_map.73) | data formatting | bytes 262144

commit v3 on v2

--- a/solution.py
+++ b/solution.py
@@ -15,8 +15,8 @@
 INFLIGHT = 3
 SUM_LAG = 2
 HIDDEN_LAG = 5
-FORWARD = 2
-EXTRA = 0
+FORWARD = 3
+EXTRA = 1
 VMEM_LIMIT = 62 * 1024 * 1024
 
 

time: 59.2 us -> 58.7 us (level)
  no operation moved by 1% of the time
where the time goes in v3:
time: 58.7 us; the launch traced here: 58.5 us
  Pallas kernels  55.5 us (95%)
  local copies, waits for them, and re-layouts  2.94 us (5%)
    pallas_call x1, Pallas kernels, body(): pl.pallas_call(make_kernel(rows, n_wide, depth, ff, chunks), out_shape=ja...  55.5 us
    unnamed x2, local copies, waits for them, and re-layouts  2.94 us

profile of v3, /device:TPU:0, one launch (start us, length us, event | category | flops | bytes accessed | tf_op | source)
XLA Modules:
  0.0 58.5 jit_solution(8028574618123997033)
XLA Ops:
  0.0 1.4 %copy.8.dkeep = s32[32,16]{1,0:T(8,128)} copy(s32[32,16]{0,1:T(8,128)} %param.13) | data formatting | bytes 4096 | tf_op args[6]
  1.4 55.5 %shard_map.73 = bf16[32,2048]{1,0:T(8,128)(2,1)} custom-call(bf16[32,2048]{1,0:T(8,128)(2,1)} %tok.1, bf16[2048,4096]{1,0:T(8,128)(2,1)} %gate.1, bf16[2048,4096]{1,0:T(8,128)(2,1)} %up.1, bf16[4096,2048]{1,0:T(8,128)(2,1)} %down.1, s32[16,32]{1,0:T(8,128)} %gkeep.1, s32[16,32]{1,0:T(8,128)} %ukeep.1, s32[32,16]{1,0:T(8,128)} %copy.8.dkeep), custom_call_target="tpu_custom_call" | custom-call | tf_op jit(solution)/shard_map/pallas_call | solution.py:305
  56.9 1.6 %copy.10 = bf16[32,2048]{1,0:T(8,128)(2,1)} copy(bf16[32,2048]{1,0:T(8,128)(2,1)} %shard_map.73) | data formatting | bytes 262144
